TPU v7x, 256 devices: a whole 4x4x8 slice. The times are simulated.
256 devices in a mesh: section: 16 (over y_hi, z), dp: 16 (over x, y_lo, core).
Axes of the slice: x: 4, y: 4 (y_hi: 2, y_lo: 2; y = y_hi * 2 + y_lo), z: 8, core: 2. Of those that a mesh axis runs over, the one named last changes fastest.
Arguments:
- parked: bfloat16 [16, 4, 512, 8192], P('section', None, 'dp'), may hold values from -40 to 40
- cotangent: bfloat16 [4, 512, 8192], P(None, 'dp'), may hold values from -12 to 12
- park_table: int32 [16, 4], replicated, may hold values from 0 to 3, each once within a row
- run_order: int32 [4], replicated, may hold values from 0 to 3, each once
- norm_gain: float32 [16, 8192], P('section'), may hold values from 0.25 to 1.75
- down_weight: bfloat16 [16, 8192, 128], P('section'), may hold values from -0.06629126 to 0.06629126
- up_weight: bfloat16 [16, 128, 8192], P('section'), may hold values from -0.13258252 to 0.13258252
Outputs:
- input_grads: bfloat16 [16, 4, 512, 8192], P('section', None, 'dp')
- grad_down: float32 [16, 8192, 128], P('section', 'dp')
- grad_up: float32 [16, 128, 8192], P('section', None, 'dp')
Inputs may be any that keep to these rules, and one draw needn't show every extreme that they name: Each row of park_table names every micro-batch once. `run_order`: names every micro-batch once.
All inputs are finite; a program needn't handle non-finite values.
Results may differ from a plain program's by a relative error of at most 0.024.
Values may be sent and summed in bfloat16 or wider, within the bound.
No kernel may reach another device: no remote copies, remote signals or barrier semaphores. Data moves between devices by JAX's collectives and lax.ppermute only.
A program may use at most 192 MiB of HBM per device.

v0:
```python
import jax
import jax.numpy as jnp
from jax import lax
from jax.sharding import PartitionSpec as P


def partner(block, axis, bit):
    count = lax.axis_size(axis)
    route = []
    for low in range(count):
        high = low | 1 << bit
        if high != low and high < count:
            route += [(low, high), (high, low)]
    return lax.ppermute(block, axis, route)


def passed_along(block, axis, distance):
    devices = range(lax.axis_size(axis))
    route = [(i - distance, i) for i in devices if i - distance in devices]
    return lax.ppermute(block, axis, route)


def layer_back(layer_in, upstream, gain_row, down_local, up_local):
    wide_in = layer_in.astype(jnp.float32)
    scale_inv = lax.rsqrt(jnp.mean(wide_in * wide_in, axis=-1, keepdims=True) + 1e-05)
    normed = wide_in * scale_inv
    hidden = (normed * gain_row).astype(jnp.bfloat16)
    pre_act = jnp.dot(hidden, down_local, preferred_element_type=jnp.float32)
    gate_sig = jax.nn.sigmoid(pre_act)
    gated_out = (pre_act * gate_sig).astype(jnp.bfloat16)
    d_gated = jnp.dot(upstream, up_local.T, preferred_element_type=jnp.float32)
    d_act = (d_gated * gate_sig * (1.0 + pre_act * (1.0 - gate_sig))).astype(jnp.bfloat16)
    d_hidden = jnp.dot(d_act, down_local.T, preferred_element_type=jnp.float32) * gain_row
    inner_mean = jnp.mean(d_hidden * normed, axis=-1, keepdims=True)
    d_input = (upstream.astype(jnp.float32) + scale_inv * (d_hidden - normed * inner_mean)).astype(
        jnp.bfloat16
    )
    return (hidden, gated_out, d_act, d_input)


def body(parked, cotangent, park_table, run_order, norm_gain, down_weight, up_weight):
    sections = lax.axis_size("section")
    own_section = lax.axis_index("section")
    bit_count = sections.bit_length() - 1
    micro_count = run_order.shape[0]
    row_count = cotangent.shape[1]
    width = cotangent.shape[2]
    gain_row = norm_gain[0]
    down_local = down_weight[0]
    up_local = up_weight[0]
    rank_width = down_local.shape[1]
    fetched = parked[0]
    hop_bits = list(range(bit_count))
    for hop_bit in hop_bits:
        fetched = partner(fetched, "section", hop_bit)
    slot_row = lax.dynamic_index_in_dim(park_table, sections - 1 - own_section, 0, keepdims=False)
    pick_slot = (run_order[:, None] == slot_row[None, :]).astype(jnp.bfloat16)
    inputs = jnp.einsum(
        "ks,srd->krd", pick_slot, fetched, preferred_element_type=jnp.float32
    ).astype(jnp.bfloat16)
    pick_micro = (run_order[:, None] == jnp.arange(micro_count, dtype=jnp.int32)[None, :]).astype(
        jnp.bfloat16
    )
    upstream_all = jnp.einsum(
        "km,mrd->krd", pick_micro, cotangent, preferred_element_type=jnp.float32
    ).astype(jnp.bfloat16)
    is_last = own_section == sections - 1

    def tick(moment, carried):
        received, grads_buf, hidden_buf, upstream_buf, gated_buf, dact_buf = carried
        position = moment - (sections - 1 - own_section)
        active = (position >= 0) & (position < micro_count)
        slot_index = jnp.clip(position, 0, micro_count - 1)
        layer_in = lax.dynamic_index_in_dim(inputs, slot_index, 0, keepdims=False)
        from_loss = lax.dynamic_index_in_dim(upstream_all, slot_index, 0, keepdims=False)
        upstream = jnp.where(is_last, from_loss, received)
        hidden, gated_out, d_act, d_input = layer_back(
            layer_in, upstream, gain_row, down_local, up_local
        )

        def store(buffer, new_value):
            previous = lax.dynamic_index_in_dim(buffer, slot_index, 0, keepdims=False)
            return lax.dynamic_update_index_in_dim(
                buffer, jnp.where(active, new_value, previous), slot_index, 0
            )

        passed = passed_along(d_input, "section", -1)
        return (
            passed,
            store(grads_buf, d_input),
            store(hidden_buf, hidden),
            store(upstream_buf, upstream),
            store(gated_buf, gated_out),
            store(dact_buf, d_act),
        )

    wide_zero = jnp.zeros((micro_count, row_count, width), jnp.bfloat16)
    thin_zero = jnp.zeros((micro_count, row_count, rank_width), jnp.bfloat16)
    initial = (
        jnp.zeros((row_count, width), jnp.bfloat16),
        wide_zero,
        wide_zero,
        wide_zero,
        thin_zero,
        thin_zero,
    )
    final_state = lax.fori_loop(0, sections + micro_count - 1, tick, initial)
    grads_buf, hidden_buf, upstream_buf, gated_buf, dact_buf = final_state[1:]
    down_terms = jnp.einsum("krd,krq->dq", hidden_buf, dact_buf, preferred_element_type=jnp.float32)
    up_terms = jnp.einsum(
        "krd,krq->dq", upstream_buf, gated_buf, preferred_element_type=jnp.float32
    )
    total_down, total_up = (
        lax.psum(down_terms.astype(jnp.bfloat16), "dp").astype(jnp.float32),
        lax.psum(up_terms.astype(jnp.bfloat16), "dp").astype(jnp.float32),
    )
    share_rows = width // lax.axis_size("dp")
    share_start = lax.axis_index("dp") * share_rows
    down_share = lax.dynamic_slice_in_dim(total_down, share_start, share_rows, 0)
    up_share = lax.dynamic_slice_in_dim(total_up, share_start, share_rows, 0)
    return (grads_buf[None], down_share[None], up_share.T[None])


def solution(mesh):
    placed = (
        P("section", None, "dp", None),
        P(None, "dp", None),
        P(),
        P(),
        P("section", None),
        P("section", None, None),
        P("section", None, None),
    )
    return jax.shard_map(
        body,
        mesh=mesh,
        in_specs=placed,
        out_specs=(
            P("section", None, "dp", None),
            P("section", "dp", None),
            P("section", None, "dp"),
        ),
        check_vma=False,
    )
```

profile of v0, /device:TPU:15, one launch (start us, length us, event | category | flops | bytes accessed | tf_op | source)
XLA Modules:
  0.0 976.8 jit_solution(4160650252122820856)
XLA Ops:
  7.2 3.3 copy.18
  12.3 45.2 %collective-permute-done.1 = bf16[4,32,8192]{2,0,1:T(4,128)(2,1)S(1)} collective-permute-done((bf16[4,32,8192]{2,0,1:T(4,128)(2,1)S(1)}, bf16[4,32,8192]{2,0,1:T(4,128)(2,1)S(1)}, u32[]{:S(2)}, u32[]{:S(2)}) %collective-permute-start.1) | collective-permute-done | bytes 2097184 | tf_op jit(solution)/shard_map/ppermute | solution.py:14
  57.5 3.0 collective-permute-start.2
  60.5 90.0 %collective-permute-done.2 = bf16[4,32,8192]{2,0,1:T(4,128)(2,1)S(1)} collective-permute-done((bf16[4,32,8192]{2,0,1:T(4,128)(2,1)S(1)}, bf16[4,32,8192]{2,0,1:T(4,128)(2,1)S(1)}, u32[]{:S(2)}, u32[]{:S(2)}) %collective-permute-start.2) | collective-permute-done | bytes 2097184 | tf_op jit(solution)/shard_map/ppermute | solution.py:14
  150.5 6.4 collective-permute-start.3
  157.0 90.5 %collective-permute-done.3 = bf16[4,32,8192]{2,0,1:T(4,128)(2,1)} collective-permute-done((bf16[4,32,8192]{2,0,1:T(4,128)(2,1)S(1)}, bf16[4,32,8192]{2,0,1:T(4,128)(2,1)}, u32[]{:S(2)}, u32[]{:S(2)}) %collective-permute-start.3) | collective-permute-done | bytes 2097184 | tf_op jit(solution)/shard_map/ppermute | solution.py:14
  249.5 2.8 convolution_convert_fusion.1
  252.3 2.5 copy.12
  255.0 39.7 %collective-permute-done.4 = bf16[4,32,8192]{2,0,1:T(4,128)(2,1)} collective-permute-done((bf16[4,32,8192]{2,0,1:T(4,128)(2,1)}, bf16[4,32,8192]{2,0,1:T(4,128)(2,1)}, u32[]{:S(2)}, u32[]{:S(2)}) %collective-permute-start.4) | collective-permute-done | bytes 2097184 | tf_op jit(solution)/shard_map/ppermute | solution.py:14
  294.8 2.9 convolution_convert_fusion
  297.7 2.5 copy.13
  304.8 472.7 %while.25 = (s32[]{:T(128)}, bf16[32,8192]{1,0:T(8,128)(2,1)S(1)}, bf16[4,32,8192]{2,1,0:T(8,128)(2,1)}, bf16[4,32,8192]{2,1,0:T(8,128)(2,1)}, bf16[4,32,8192]{2...) while((s32[]{:T(128)}, bf16[32,8192]{1,0:T(8,128)(2,1)S(1)}, ...), condition=%wide.region_3.4_spmd, body=%wide.region_0.3_spmd.sunk | while | flops 208470048 | bytes 46357236 | solution.py:107
  309.5 2.4 bitcast_dynamic-update-slice_fusion.8
  314.4 2.6 bitcast_dynamic-update-slice_fusion.11
  318.3 11.4 %collective-permute-done = bf16[32,8192]{1,0:T(8,128)(2,1)S(1)} collective-permute-done((bf16[32,8192]{1,0:T(8,128)(2,1)S(1)}, bf16[32,8192]{1,0:T(8,128)(2,1)S(1)}, u32[]{:S(2)}, u32[]{:S(2)}) %collective-permute-start) | collective-permute-done | bytes 524320 | tf_op jit(solution)/shard_map/while/body/eval_jaxpr/ppermute | solution.py:20
  334.4 2.4 bitcast_dynamic-update-slice_fusion.8
  339.4 2.6 bitcast_dynamic-update-slice_fusion.11
  343.2 10.5 %collective-permute-done = bf16[32,8192]{1,0:T(8,128)(2,1)S(1)} collective-permute-done((bf16[32,8192]{1,0:T(8,128)(2,1)S(1)}, bf16[32,8192]{1,0:T(8,128)(2,1)S(1)}, u32[]{:S(2)}, u32[]{:S(2)}) %collective-permute-start) | collective-permute-done | bytes 524320 | tf_op jit(solution)/shard_map/while/body/eval_jaxpr/ppermute | solution.py:20
  363.3 2.6 bitcast_dynamic-update-slice_fusion.11
  367.2 12.5 %collective-permute-done = bf16[32,8192]{1,0:T(8,128)(2,1)S(1)} collective-permute-done((bf16[32,8192]{1,0:T(8,128)(2,1)S(1)}, bf16[32,8192]{1,0:T(8,128)(2,1)S(1)}, u32[]{:S(2)}, u32[]{:S(2)}) %collective-permute-start) | collective-permute-done | bytes 524320 | tf_op jit(solution)/shard_map/while/body/eval_jaxpr/ppermute | solution.py:20
  384.4 2.4 bitcast_dynamic-update-slice_fusion.8
  389.4 2.6 bitcast_dynamic-update-slice_fusion.11
  393.2 10.3 %collective-permute-done = bf16[32,8192]{1,0:T(8,128)(2,1)S(1)} collective-permute-done((bf16[32,8192]{1,0:T(8,128)(2,1)S(1)}, bf16[32,8192]{1,0:T(8,128)(2,1)S(1)}, u32[]{:S(2)}, u32[]{:S(2)}) %collective-permute-start) | collective-permute-done | bytes 524320 | tf_op jit(solution)/shard_map/while/body/eval_jaxpr/ppermute | solution.py:20
  413.2 2.6 bitcast_dynamic-update-slice_fusion.11
  417.0 9.4 collective-permute-done
  431.1 2.4 bitcast_dynamic-update-slice_fusion.8
  436.0 2.6 bitcast_dynamic-update-slice_fusion.11
  439.9 8.9 collective-permute-done
  458.4 2.6 bitcast_dynamic-update-slice_fusion.11
  462.3 9.6 collective-permute-done
  481.5 2.6 bitcast_dynamic-update-slice_fusion.11
  485.3 11.0 %collective-permute-done = bf16[32,8192]{1,0:T(8,128)(2,1)S(1)} collective-permute-done((bf16[32,8192]{1,0:T(8,128)(2,1)S(1)}, bf16[32,8192]{1,0:T(8,128)(2,1)S(1)}, u32[]{:S(2)}, u32[]{:S(2)}) %collective-permute-start) | collective-permute-done | bytes 524320 | tf_op jit(solution)/shard_map/while/body/eval_jaxpr/ppermute | solution.py:20
  501.0 2.4 bitcast_dynamic-update-slice_fusion.8
  506.0 2.6 bitcast_dynamic-update-slice_fusion.11
  509.9 12.6 %collective-permute-done = bf16[32,8192]{1,0:T(8,128)(2,1)S(1)} collective-permute-done((bf16[32,8192]{1,0:T(8,128)(2,1)S(1)}, bf16[32,8192]{1,0:T(8,128)(2,1)S(1)}, u32[]{:S(2)}, u32[]{:S(2)}) %collective-permute-start) | collective-permute-done | bytes 524320 | tf_op jit(solution)/shard_map/while/body/eval_jaxpr/ppermute | solution.py:20
  527.2 2.4 bitcast_dynamic-update-slice_fusion.8
  532.1 2.6 bitcast_dynamic-update-slice_fusion.11
  536.0 10.9 %collective-permute-done = bf16[32,8192]{1,0:T(8,128)(2,1)S(1)} collective-permute-done((bf16[32,8192]{1,0:T(8,128)(2,1)S(1)}, bf16[32,8192]{1,0:T(8,128)(2,1)S(1)}, u32[]{:S(2)}, u32[]{:S(2)}) %collective-permute-start) | collective-permute-done | bytes 524320 | tf_op jit(solution)/shard_map/while/body/eval_jaxpr/ppermute | solution.py:20
  551.6 2.4 bitcast_dynamic-update-slice_fusion.8
  556.5 2.6 bitcast_dynamic-update-slice_fusion.11
  560.4 11.7 %collective-permute-done = bf16[32,8192]{1,0:T(8,128)(2,1)S(1)} collective-permute-done((bf16[32,8192]{1,0:T(8,128)(2,1)S(1)}, bf16[32,8192]{1,0:T(8,128)(2,1)S(1)}, u32[]{:S(2)}, u32[]{:S(2)}) %collective-permute-start) | collective-permute-done | bytes 524320 | tf_op jit(solution)/shard_map/while/body/eval_jaxpr/ppermute | solution.py:20
  576.8 2.4 bitcast_dynamic-update-slice_fusion.8
  581.7 2.6 bitcast_dynamic-update-slice_fusion.11
  585.6 11.7 %collective-permute-done = bf16[32,8192]{1,0:T(8,128)(2,1)S(1)} collective-permute-done((bf16[32,8192]{1,0:T(8,128)(2,1)S(1)}, bf16[32,8192]{1,0:T(8,128)(2,1)S(1)}, u32[]{:S(2)}, u32[]{:S(2)}) %collective-permute-start) | collective-permute-done | bytes 524320 | tf_op jit(solution)/shard_map/while/body/eval_jaxpr/ppermute | solution.py:20
  606.9 2.6 bitcast_dynamic-update-slice_fusion.11
  610.8 12.2 %collective-permute-done = bf16[32,8192]{1,0:T(8,128)(2,1)S(1)} collective-permute-done((bf16[32,8192]{1,0:T(8,128)(2,1)S(1)}, bf16[32,8192]{1,0:T(8,128)(2,1)S(1)}, u32[]{:S(2)}, u32[]{:S(2)}) %collective-permute-start) | collective-permute-done | bytes 524320 | tf_op jit(solution)/shard_map/while/body/eval_jaxpr/ppermute | solution.py:20
  632.6 2.6 bitcast_dynamic-update-slice_fusion.11
  636.5 12.2 %collective-permute-done = bf16[32,8192]{1,0:T(8,128)(2,1)S(1)} collective-permute-done((bf16[32,8192]{1,0:T(8,128)(2,1)S(1)}, bf16[32,8192]{1,0:T(8,128)(2,1)S(1)}, u32[]{:S(2)}, u32[]{:S(2)}) %collective-permute-start) | collective-permute-done | bytes 524320 | tf_op jit(solution)/shard_map/while/body/eval_jaxpr/ppermute | solution.py:20
  653.4 2.4 bitcast_dynamic-update-slice_fusion.8
  658.3 2.6 bitcast_dynamic-update-slice_fusion.11
  662.2 12.2 %collective-permute-done = bf16[32,8192]{1,0:T(8,128)(2,1)S(1)} collective-permute-done((bf16[32,8192]{1,0:T(8,128)(2,1)S(1)}, bf16[32,8192]{1,0:T(8,128)(2,1)S(1)}, u32[]{:S(2)}, u32[]{:S(2)}) %collective-permute-start) | collective-permute-done | bytes 524320 | tf_op jit(solution)/shard_map/while/body/eval_jaxpr/ppermute | solution.py:20
  679.1 2.4 bitcast_dynamic-update-slice_fusion.8
  684.1 2.6 bitcast_dynamic-update-slice_fusion.11
  688.0 12.2 %collective-permute-done = bf16[32,8192]{1,0:T(8,128)(2,1)S(1)} collective-permute-done((bf16[32,8192]{1,0:T(8,128)(2,1)S(1)}, bf16[32,8192]{1,0:T(8,128)(2,1)S(1)}, u32[]{:S(2)}, u32[]{:S(2)}) %collective-permute-start) | collective-permute-done | bytes 524320 | tf_op jit(solution)/shard_map/while/body/eval_jaxpr/ppermute | solution.py:20
  709.8 2.6 bitcast_dynamic-update-slice_fusion.11
  713.7 12.3 %collective-permute-done = bf16[32,8192]{1,0:T(8,128)(2,1)S(1)} collective-permute-done((bf16[32,8192]{1,0:T(8,128)(2,1)S(1)}, bf16[32,8192]{1,0:T(8,128)(2,1)S(1)}, u32[]{:S(2)}, u32[]{:S(2)}) %collective-permute-start) | collective-permute-done | bytes 524320 | tf_op jit(solution)/shard_map/while/body/eval_jaxpr/ppermute | solution.py:20
  730.6 2.4 bitcast_dynamic-update-slice_fusion.8
  735.6 2.6 bitcast_dynamic-update-slice_fusion.11
  739.4 12.4 %collective-permute-done = bf16[32,8192]{1,0:T(8,128)(2,1)S(1)} collective-permute-done((bf16[32,8192]{1,0:T(8,128)(2,1)S(1)}, bf16[32,8192]{1,0:T(8,128)(2,1)S(1)}, u32[]{:S(2)}, u32[]{:S(2)}) %collective-permute-start) | collective-permute-done | bytes 524320 | tf_op jit(solution)/shard_map/while/body/eval_jaxpr/ppermute | solution.py:20
  756.5 2.4 bitcast_dynamic-update-slice_fusion.8
  761.4 2.6 bitcast_dynamic-update-slice_fusion.11
  765.3 12.2 %collective-permute-done = bf16[32,8192]{1,0:T(8,128)(2,1)S(1)} collective-permute-done((bf16[32,8192]{1,0:T(8,128)(2,1)S(1)}, bf16[32,8192]{1,0:T(8,128)(2,1)S(1)}, u32[]{:S(2)}, u32[]{:S(2)}) %collective-permute-start) | collective-permute-done | bytes 524320 | tf_op jit(solution)/shard_map/while/body/eval_jaxpr/ppermute | solution.py:20
  777.6 3.8 fusion.26
  783.5 183.8 %all-reduce.3.cloned.1.call-done = (bf16[8192,128]{1,0:T(8,128)(2,1)}, bf16[8192,128]{1,0:T(8,128)(2,1)}) async-done(((bf16[8192,128]{1,0:T(8,128)(2,1)}, bf16[8192,128]{1,0:T(8,128)(2,1)}), (bf16[8192,128]{1,0:T(8,128)(2,1)}, bf16[8192,128]{1,0:T(8,128)(2,1)})) %all-reduce.3.cloned.1.call-update) | async-done | bytes 4194320 | tf_op jit(solution)/shard_map/psum | solution.py:114
  (316 shorter events, 190.9 us)
Async XLA Ops:
  7.2 242.4 %copy-start = (bf16[4,32,8192]{2,1,0:T(8,128)(2,1)S(1)}, bf16[4,32,8192]{2,1,0:T(8,128)(2,1)}, u32[]{:S(2)}) copy-start(bf16[4,32,8192]{2,1,0:T(8,128)(2,1)} %param.10) | copy-start | bytes 6291460
  7.2 242.3 %copy-start.7 = (s32[4]{0:T(128)S(1)}, s32[4]{0:T(128)}, u32[]{:S(2)}) copy-start(s32[4]{0:T(128)} %param.12) | copy-start | bytes 52
  7.2 960.2 %all-reduce.3.cloned.1.call-start = ((), (), s32[]{:S(2)}) async-start(), calls=%async_computation | async-start | bytes 8388608 | tf_op jit(solution)/shard_map/psum | solution.py:114
  10.6 47.0 %collective-permute-start.1 = (bf16[4,32,8192]{2,0,1:T(4,128)(2,1)S(1)}, bf16[4,32,8192]{2,0,1:T(4,128)(2,1)S(1)}, u32[]{:S(2)}, u32[]{:S(2)}) collective-permute-start(bf16[4,32,8192]{2,0,1:T(4,128)(2,1)S(1)} %bitcast.134), channel_id=1, source_target_pairs={{0,16},{16,0},{32,48},{48,32},{64,80},{80,64},{96,112},{112,96},{1... | collective-permute-start | bytes 6291464 | tf_op jit(solution)/shard_map/ppermute | solution.py:14
  57.5 93.0 %collective-permute-start.2 = (bf16[4,32,8192]{2,0,1:T(4,128)(2,1)S(1)}, bf16[4,32,8192]{2,0,1:T(4,128)(2,1)S(1)}, u32[]{:S(2)}, u32[]{:S(2)}) collective-permute-start(bf16[4,32,8192]{2,0,1:T(4,128)(2,1)S(1)} %collective-permute-done.1), channel_id=1, source_target_pairs={{0,32},{32,0},{16,48},{48,16},{64,96},{96,64},{80,112},{112,80},{1... | collective-permute-start | bytes 6291464 | tf_op jit(solution)/shard_map/ppermute | solution.py:14
  150.5 97.0 %collective-permute-start.3 = (bf16[4,32,8192]{2,0,1:T(4,128)(2,1)S(1)}, bf16[4,32,8192]{2,0,1:T(4,128)(2,1)}, u32[]{:S(2)}, u32[]{:S(2)}) collective-permute-start(bf16[4,32,8192]{2,0,1:T(4,128)(2,1)S(1)} %collective-permute-done.2), channel_id=1, source_target_pairs={{0,64},{64,0},{16,80},{80,16},{32,96},{96,32},{48,112},{112,48},{1... | collective-permute-start | bytes 6291464 | tf_op jit(solution)/shard_map/ppermute | solution.py:14
  247.5 47.3 %collective-permute-start.4 = (bf16[4,32,8192]{2,0,1:T(4,128)(2,1)}, bf16[4,32,8192]{2,0,1:T(4,128)(2,1)}, u32[]{:S(2)}, u32[]{:S(2)}) collective-permute-start(bf16[4,32,8192]{2,0,1:T(4,128)(2,1)} %collective-permute-done.3), channel_id=1, source_target_pairs={{0,128},{128,0},{16,144},{144,16},{32,160},{160,32},{48,176},{176,... | collective-permute-start | bytes 6291464 | tf_op jit(solution)/shard_map/ppermute | solution.py:14
  252.3 2.5 copy-start.6
  301.8 3.1 copy-start.5
  309.5 2.4 copy-start.3
  309.5 3.2 copy-start.2
  317.0 12.7 %collective-permute-start = (bf16[32,8192]{1,0:T(8,128)(2,1)S(1)}, bf16[32,8192]{1,0:T(8,128)(2,1)S(1)}, u32[]{:S(2)}, u32[]{:S(2)}) collective-permute-start(bf16[32,8192]{1,0:T(8,128)(2,1)S(1)} %get-tuple-element.499), channel_id=1, source_target_pairs={{16,0},{32,16},{48,32},{64,48},{80,64},{96,80},{112,96},{128,112},... | collective-permute-start | bytes 1572872 | tf_op jit(solution)/shard_map/while/body/eval_jaxpr/ppermute | solution.py:20
  334.4 2.4 copy-start.3
  334.4 3.2 copy-start.2
  341.9 11.8 %collective-permute-start = (bf16[32,8192]{1,0:T(8,128)(2,1)S(1)}, bf16[32,8192]{1,0:T(8,128)(2,1)S(1)}, u32[]{:S(2)}, u32[]{:S(2)}) collective-permute-start(bf16[32,8192]{1,0:T(8,128)(2,1)S(1)} %get-tuple-element.499), channel_id=1, source_target_pairs={{16,0},{32,16},{48,32},{64,48},{80,64},{96,80},{112,96},{128,112},... | collective-permute-start | bytes 1572872 | tf_op jit(solution)/shard_map/while/body/eval_jaxpr/ppermute | solution.py:20
  358.4 2.4 copy-start.3
  358.4 3.2 copy-start.2
  365.9 13.8 %collective-permute-start = (bf16[32,8192]{1,0:T(8,128)(2,1)S(1)}, bf16[32,8192]{1,0:T(8,128)(2,1)S(1)}, u32[]{:S(2)}, u32[]{:S(2)}) collective-permute-start(bf16[32,8192]{1,0:T(8,128)(2,1)S(1)} %get-tuple-element.499), channel_id=1, source_target_pairs={{16,0},{32,16},{48,32},{64,48},{80,64},{96,80},{112,96},{128,112},... | collective-permute-start | bytes 1572872 | tf_op jit(solution)/shard_map/while/body/eval_jaxpr/ppermute | solution.py:20
  384.4 2.4 copy-start.3
  384.4 3.2 copy-start.2
  392.0 11.6 %collective-permute-start = (bf16[32,8192]{1,0:T(8,128)(2,1)S(1)}, bf16[32,8192]{1,0:T(8,128)(2,1)S(1)}, u32[]{:S(2)}, u32[]{:S(2)}) collective-permute-start(bf16[32,8192]{1,0:T(8,128)(2,1)S(1)} %get-tuple-element.499), channel_id=1, source_target_pairs={{16,0},{32,16},{48,32},{64,48},{80,64},{96,80},{112,96},{128,112},... | collective-permute-start | bytes 1572872 | tf_op jit(solution)/shard_map/while/body/eval_jaxpr/ppermute | solution.py:20
  408.2 2.4 copy-start.3
  408.2 3.2 copy-start.2
  415.7 10.7 %collective-permute-start = (bf16[32,8192]{1,0:T(8,128)(2,1)S(1)}, bf16[32,8192]{1,0:T(8,128)(2,1)S(1)}, u32[]{:S(2)}, u32[]{:S(2)}) collective-permute-start(bf16[32,8192]{1,0:T(8,128)(2,1)S(1)} %get-tuple-element.499), channel_id=1, source_target_pairs={{16,0},{32,16},{48,32},{64,48},{80,64},{96,80},{112,96},{128,112},... | collective-permute-start | bytes 1572872 | tf_op jit(solution)/shard_map/while/body/eval_jaxpr/ppermute | solution.py:20
  431.1 2.4 copy-start.3
  431.1 3.2 copy-start.2
  438.6 10.2 %collective-permute-start = (bf16[32,8192]{1,0:T(8,128)(2,1)S(1)}, bf16[32,8192]{1,0:T(8,128)(2,1)S(1)}, u32[]{:S(2)}, u32[]{:S(2)}) collective-permute-start(bf16[32,8192]{1,0:T(8,128)(2,1)S(1)} %get-tuple-element.499), channel_id=1, source_target_pairs={{16,0},{32,16},{48,32},{64,48},{80,64},{96,80},{112,96},{128,112},... | collective-permute-start | bytes 1572872 | tf_op jit(solution)/shard_map/while/body/eval_jaxpr/ppermute | solution.py:20
  453.4 2.4 copy-start.3
  453.5 3.2 copy-start.2
  461.0 10.8 %collective-permute-start = (bf16[32,8192]{1,0:T(8,128)(2,1)S(1)}, bf16[32,8192]{1,0:T(8,128)(2,1)S(1)}, u32[]{:S(2)}, u32[]{:S(2)}) collective-permute-start(bf16[32,8192]{1,0:T(8,128)(2,1)S(1)} %get-tuple-element.499), channel_id=1, source_target_pairs={{16,0},{32,16},{48,32},{64,48},{80,64},{96,80},{112,96},{128,112},... | collective-permute-start | bytes 1572872 | tf_op jit(solution)/shard_map/while/body/eval_jaxpr/ppermute | solution.py:20
  476.5 2.4 copy-start.3
  476.5 3.2 copy-start.2
  484.1 12.3 %collective-permute-start = (bf16[32,8192]{1,0:T(8,128)(2,1)S(1)}, bf16[32,8192]{1,0:T(8,128)(2,1)S(1)}, u32[]{:S(2)}, u32[]{:S(2)}) collective-permute-start(bf16[32,8192]{1,0:T(8,128)(2,1)S(1)} %get-tuple-element.499), channel_id=1, source_target_pairs={{16,0},{32,16},{48,32},{64,48},{80,64},{96,80},{112,96},{128,112},... | collective-permute-start | bytes 1572872 | tf_op jit(solution)/shard_map/while/body/eval_jaxpr/ppermute | solution.py:20
  501.0 2.4 copy-start.3
  501.0 3.2 copy-start.2
  508.6 13.9 %collective-permute-start = (bf16[32,8192]{1,0:T(8,128)(2,1)S(1)}, bf16[32,8192]{1,0:T(8,128)(2,1)S(1)}, u32[]{:S(2)}, u32[]{:S(2)}) collective-permute-start(bf16[32,8192]{1,0:T(8,128)(2,1)S(1)} %get-tuple-element.499), channel_id=1, source_target_pairs={{16,0},{32,16},{48,32},{64,48},{80,64},{96,80},{112,96},{128,112},... | collective-permute-start | bytes 1572872 | tf_op jit(solution)/shard_map/while/body/eval_jaxpr/ppermute | solution.py:20
  527.1 2.4 copy-start.3
  527.1 3.2 copy-start.2
  534.7 12.2 %collective-permute-start = (bf16[32,8192]{1,0:T(8,128)(2,1)S(1)}, bf16[32,8192]{1,0:T(8,128)(2,1)S(1)}, u32[]{:S(2)}, u32[]{:S(2)}) collective-permute-start(bf16[32,8192]{1,0:T(8,128)(2,1)S(1)} %get-tuple-element.499), channel_id=1, source_target_pairs={{16,0},{32,16},{48,32},{64,48},{80,64},{96,80},{112,96},{128,112},... | collective-permute-start | bytes 1572872 | tf_op jit(solution)/shard_map/while/body/eval_jaxpr/ppermute | solution.py:20
  551.6 3.2 copy-start.2
  559.1 13.0 %collective-permute-start = (bf16[32,8192]{1,0:T(8,128)(2,1)S(1)}, bf16[32,8192]{1,0:T(8,128)(2,1)S(1)}, u32[]{:S(2)}, u32[]{:S(2)}) collective-permute-start(bf16[32,8192]{1,0:T(8,128)(2,1)S(1)} %get-tuple-element.499), channel_id=1, source_target_pairs={{16,0},{32,16},{48,32},{64,48},{80,64},{96,80},{112,96},{128,112},... | collective-permute-start | bytes 1572872 | tf_op jit(solution)/shard_map/while/body/eval_jaxpr/ppermute | solution.py:20
  576.7 2.4 copy-start.3
  576.7 3.2 copy-start.2
  584.3 13.0 %collective-permute-start = (bf16[32,8192]{1,0:T(8,128)(2,1)S(1)}, bf16[32,8192]{1,0:T(8,128)(2,1)S(1)}, u32[]{:S(2)}, u32[]{:S(2)}) collective-permute-start(bf16[32,8192]{1,0:T(8,128)(2,1)S(1)} %get-tuple-element.499), channel_id=1, source_target_pairs={{16,0},{32,16},{48,32},{64,48},{80,64},{96,80},{112,96},{128,112},... | collective-permute-start | bytes 1572872 | tf_op jit(solution)/shard_map/while/body/eval_jaxpr/ppermute | solution.py:20
  601.9 2.4 copy-start.3
  601.9 3.2 copy-start.2
  609.5 13.5 %collective-permute-start = (bf16[32,8192]{1,0:T(8,128)(2,1)S(1)}, bf16[32,8192]{1,0:T(8,128)(2,1)S(1)}, u32[]{:S(2)}, u32[]{:S(2)}) collective-permute-start(bf16[32,8192]{1,0:T(8,128)(2,1)S(1)} %get-tuple-element.499), channel_id=1, source_target_pairs={{16,0},{32,16},{48,32},{64,48},{80,64},{96,80},{112,96},{128,112},... | collective-permute-start | bytes 1572872 | tf_op jit(solution)/shard_map/while/body/eval_jaxpr/ppermute | solution.py:20
  627.7 3.2 copy-start.2
  635.2 13.5 %collective-permute-start = (bf16[32,8192]{1,0:T(8,128)(2,1)S(1)}, bf16[32,8192]{1,0:T(8,128)(2,1)S(1)}, u32[]{:S(2)}, u32[]{:S(2)}) collective-permute-start(bf16[32,8192]{1,0:T(8,128)(2,1)S(1)} %get-tuple-element.499), channel_id=1, source_target_pairs={{16,0},{32,16},{48,32},{64,48},{80,64},{96,80},{112,96},{128,112},... | collective-permute-start | bytes 1572872 | tf_op jit(solution)/shard_map/while/body/eval_jaxpr/ppermute | solution.py:20
  653.4 2.4 copy-start.3
  653.4 3.2 copy-start.2
  660.9 13.5 %collective-permute-start = (bf16[32,8192]{1,0:T(8,128)(2,1)S(1)}, bf16[32,8192]{1,0:T(8,128)(2,1)S(1)}, u32[]{:S(2)}, u32[]{:S(2)}) collective-permute-start(bf16[32,8192]{1,0:T(8,128)(2,1)S(1)} %get-tuple-element.499), channel_id=1, source_target_pairs={{16,0},{32,16},{48,32},{64,48},{80,64},{96,80},{112,96},{128,112},... | collective-permute-start | bytes 1572872 | tf_op jit(solution)/shard_map/while/body/eval_jaxpr/ppermute | solution.py:20
  679.1 2.4 copy-start.3
  679.1 3.2 copy-start.2
  686.7 13.5 %collective-permute-start = (bf16[32,8192]{1,0:T(8,128)(2,1)S(1)}, bf16[32,8192]{1,0:T(8,128)(2,1)S(1)}, u32[]{:S(2)}, u32[]{:S(2)}) collective-permute-start(bf16[32,8192]{1,0:T(8,128)(2,1)S(1)} %get-tuple-element.499), channel_id=1, source_target_pairs={{16,0},{32,16},{48,32},{64,48},{80,64},{96,80},{112,96},{128,112},... | collective-permute-start | bytes 1572872 | tf_op jit(solution)/shard_map/while/body/eval_jaxpr/ppermute | solution.py:20
  704.8 3.2 copy-start.2
  712.4 13.6 %collective-permute-start = (bf16[32,8192]{1,0:T(8,128)(2,1)S(1)}, bf16[32,8192]{1,0:T(8,128)(2,1)S(1)}, u32[]{:S(2)}, u32[]{:S(2)}) collective-permute-start(bf16[32,8192]{1,0:T(8,128)(2,1)S(1)} %get-tuple-element.499), channel_id=1, source_target_pairs={{16,0},{32,16},{48,32},{64,48},{80,64},{96,80},{112,96},{128,112},... | collective-permute-start | bytes 1572872 | tf_op jit(solution)/shard_map/while/body/eval_jaxpr/ppermute | solution.py:20
  730.6 2.4 copy-start.3
  730.6 3.2 copy-start.2
  738.1 13.7 %collective-permute-start = (bf16[32,8192]{1,0:T(8,128)(2,1)S(1)}, bf16[32,8192]{1,0:T(8,128)(2,1)S(1)}, u32[]{:S(2)}, u32[]{:S(2)}) collective-permute-start(bf16[32,8192]{1,0:T(8,128)(2,1)S(1)} %get-tuple-element.499), channel_id=1, source_target_pairs={{16,0},{32,16},{48,32},{64,48},{80,64},{96,80},{112,96},{128,112},... | collective-permute-start | bytes 1572872 | tf_op jit(solution)/shard_map/while/body/eval_jaxpr/ppermute | solution.py:20
  756.5 2.4 copy-start.3
  756.5 3.2 copy-start.2
  764.0 13.5 %collective-permute-start = (bf16[32,8192]{1,0:T(8,128)(2,1)S(1)}, bf16[32,8192]{1,0:T(8,128)(2,1)S(1)}, u32[]{:S(2)}, u32[]{:S(2)}) collective-permute-start(bf16[32,8192]{1,0:T(8,128)(2,1)S(1)} %get-tuple-element.499), channel_id=1, source_target_pairs={{16,0},{32,16},{48,32},{64,48},{80,64},{96,80},{112,96},{128,112},... | collective-permute-start | bytes 1572872 | tf_op jit(solution)/shard_map/while/body/eval_jaxpr/ppermute | solution.py:20
  777.6 3.8 copy-start.4
  (22 other events, 38.1 us)
Sparse Core Ops, SparseCore 0:
  783.6 183.6 all-reduce.2
where the time goes:
time: 981 us; the launch traced here: 977 us
  waiting for transfers between devices  666 us (68%)
  other arithmetic  120 us (12%)
  matrix products  88.4 us (9%)
  local copies, waits for them, and re-layouts  49.9 us (5%)
  starting transfers between devices  37.5 us (4%)
  between operations  14.1 us (1%)
    ppermute x4, waiting for transfers between devices, partner(): return lax.ppermute(block, axis, route)  266 us
    ppermute x19, waiting for transfers between devices, passed_along(): return lax.ppermute(block, axis, route)  216 us
    psum x1, waiting for transfers between devices, body(): lax.psum(down_terms.astype(jnp.bfloat16), 'dp').astype(jnp.float32)  184 us
    dynamic_update_slice x38, other arithmetic, store(): lax.dynamic_update_index_in_dim(buffer, jnp.where(active, new_value, prev...  94.1 us
    dot_general x19, matrix products, layer_back(): pre_act = jnp.dot(hidden, down_local, preferred_element_type=jnp.float32)  43.2 us
    ppermute x19, starting transfers between devices, passed_along(): return lax.ppermute(block, axis, route)  24.3 us
    reduce_sum x19, other arithmetic, layer_back(): jnp.mean(wide_in * wide_in, axis=-1, keepdims=True) + 1e-05  23.7 us
    dynamic_slice x38, local copies, waits for them, and re-layouts, store(): previous = lax.dynamic_index_in_dim(buffer, slot_index, 0, keepdims=False)  20.9 us
  transfers between devices with their start and end apart: 24, of which 24 were waited for; matrix products, arithmetic and copies ran while one was open for 1% of the time, Pallas kernels for 0%

commit v1 on v0

v1 whole, which is shorter than its diff:
```python
import functools
import jax
import jax.numpy as jnp
from jax import lax
from jax.experimental import pallas as pl
from jax.experimental.pallas import tpu as pltpu
from jax.sharding import PartitionSpec as P

N = 16
BLK = 8
ROWS = 128
ROWN = ROWS // N
F = 512
RANK = 128
WIDTH = N * F
PAIRS = [(j, i) for j in range(BLK - 1, 0, -1) for i in range(j)]
PAIR_AT = {pair: n for n, pair in enumerate(PAIRS)}
NP = len(PAIRS)
VMEM = 56 << 20
BF = jnp.bfloat16
F32 = jnp.float32

NT = (((1,), (1,)), ((), ()))
NN = (((1,), (0,)), ((), ()))
TN = (((0,), (0,)), ((), ()))


def dot(a, b, dims):
    return lax.dot_general(a, b, dims, preferred_element_type=F32)


def cols(m, n=1):
    return slice(m * RANK, (m + n) * RANK)


def call(kernel, outs, **kw):
    return pl.pallas_call(
        kernel,
        out_shape=[jax.ShapeDtypeStruct(s, d) for s, d in outs],
        compiler_params=pltpu.CompilerParams(vmem_limit_bytes=VMEM),
        **kw,
    )


def split_kernel(slots, src, dst):
    for n in range(N):
        dst[n, 0] = src[0, :, n * F : (n + 1) * F]


def split_rows(parked, slots):
    micro, rows, width = parked.shape
    return pl.pallas_call(
        split_kernel,
        grid_spec=pltpu.PrefetchScalarGridSpec(
            num_scalar_prefetch=1,
            grid=(micro,),
            in_specs=[pl.BlockSpec((1, rows, width), lambda k, slots: (slots[k], 0, 0))],
            out_specs=pl.BlockSpec((N, 1, rows, F), lambda k, slots: (0, k, 0, 0)),
        ),
        out_shape=jax.ShapeDtypeStruct((N, micro, rows, F), BF),
        compiler_params=pltpu.CompilerParams(vmem_limit_bytes=VMEM),
    )(slots, parked).reshape(N, micro * rows, F)


def join_kernel(src, dst):
    for n in range(N):
        dst[0, :, n * F : (n + 1) * F] = src[n, 0]


def join_rows(pieces, micro):
    rows = ROWS // micro
    return pl.pallas_call(
        join_kernel,
        grid=(micro,),
        in_specs=[pl.BlockSpec((N, 1, rows, F), lambda k: (0, k, 0, 0))],
        out_specs=pl.BlockSpec((1, rows, N * F), lambda k: (k, 0, 0)),
        out_shape=jax.ShapeDtypeStruct((micro, rows, N * F), BF),
        compiler_params=pltpu.CompilerParams(vmem_limit_bytes=VMEM),
    )(pieces.reshape(N, micro, rows, F))


def weight_kernel(jx, ix, big, up, down, part):
    for s in range(N):
        for p in range(N):
            r, h = p // 2, p % 2
            for c in range(2):
                at = (2 * h + c) * RANK
                up[s, 16 * r : 16 * r + 16, at : at + RANK] = big[p, s, 16 * c : 16 * c + 16, :]
            down[s, 32 * p : 32 * p + 32, :] = big[p, s, 32:64, :]
    for d in range(4):
        part[RANK * d : RANK * (d + 1), :] = dot(down[jx[d]].T, up[ix[d]], NT).astype(BF)


def cross_kernel(first, xs, up, down, *refs):
    base = BLK if first else 0
    cot, pay = refs if first else (None, refs[0])
    at = 0

    def ups(n):
        return up[base : base + n].reshape(n * RANK, F)

    if first:
        pay[:, cols(0, BLK)] = dot(cot[...], ups(BLK), NT).astype(BF)
        at = BLK
    for t in range(BLK):
        pay[:, cols(at + t)] = dot(xs[N - 1 - base - t], down[base + t], NN).astype(BF)
    at += BLK
    for j in range(BLK - 1, 0, -1):
        pay[:, cols(at, j)] = dot(xs[N - 1 - base - j], ups(j), NT).astype(BF)
        at += j
    if first:
        lane = lax.broadcasted_iota(jnp.int32, (ROWS, RANK), 1)
        total = jnp.zeros((ROWS, RANK), F32)
        for s in range(N):
            wide = xs[N - 1 - s].astype(F32)
            power = jnp.sum(wide * wide, axis=1, keepdims=True)
            high = power.astype(BF).astype(F32)
            total = jnp.where(lane == s, high, total)
            total = jnp.where(lane == N + s, power - high, total)
        pay[:, cols(at)] = total.astype(BF)


def rank_kernel(first, *refs):
    if first:
        sums, weights, coef, gates = refs
        c_ref, a_ref, p_ref = sums, sums, sums
        a_at, x_at, p_at, base = BLK, 2 * BLK, 2 * BLK + NP, BLK
    else:
        c_ref, a_ref, p_ref, weights, coef, gates = refs
        a_at, x_at, p_at, base = 0, BLK, 0, 0

    def total(ref, m, n=1):
        return jnp.sum(ref[:, cols(m, n)].astype(F32).reshape(N, ROWN, n * RANK), axis=0)

    power = total(p_ref, p_at)
    grads = [total(c_ref, t) for t in range(BLK)]
    lane = lax.broadcasted_iota(jnp.int32, (ROWN, RANK), 1)
    shares = jnp.zeros((ROWN, RANK), F32)
    cross_at = x_at
    for j in range(BLK - 1, -1, -1):
        s = base + j
        mean = (power[:, s : s + 1] + power[:, N + s : N + s + 1]) * (1.0 / WIDTH)
        scale = lax.rsqrt(mean + 1e-05)
        act = total(a_ref, a_at + j) * scale
        sig = jax.nn.sigmoid(act)
        gates[:, cols(j)] = jnp.tile(act * sig, (N, 1)).astype(BF)
        d_act = grads[j] * sig * (1.0 + act * (1.0 - sig))
        inner = jnp.sum(d_act * act, axis=1, keepdims=True) * (1.0 / WIDTH)
        sent = (d_act * scale).astype(BF)
        share = (inner * scale * scale).astype(BF).astype(F32)
        coef[:, cols(j)] = jnp.tile(d_act * scale, (N, 1)).astype(BF)
        shares = jnp.where(lane == j, share, shares)
        if j:
            mats = []
            for i in range(j):
                gap = j - i
                p, d = (i, gap) if gap <= 4 else (j, BLK - gap)
                mats.append(weights[base + p, RANK * (d - 1) : RANK * d, :])
            step = dot(sent, jnp.concatenate(mats, axis=1), NN)
            step = step - share * total(a_ref, cross_at, j)
            cross_at += j
            for i in range(j):
                grads[i] = grads[i] + step[:, cols(i)]
    coef[:, cols(BLK)] = jnp.tile(shares, (N, 1)).astype(BF)


def update_kernel(first, top, coef, xs, down, *refs):
    base = BLK if first else 0
    if first:
        up, out, pay, carry = refs
    else:
        _, out = refs
    grad = top[...].astype(F32)
    shares = coef[:, cols(BLK)].astype(F32)
    for j in range(BLK - 1, -1, -1):
        low = dot(coef[:, cols(j)], down[j], NT)
        grad = grad + low - shares[:, j : j + 1] * xs[BLK - 1 - j].astype(F32)
        out[j] = grad.astype(BF)
    if first:
        carry[...] = grad
        pay[...] = dot(grad.astype(BF), up[...].reshape(BLK * RANK, F), NT).astype(BF)


def parts_kernel(coef, gates, xs, top, grads, parts):
    for j in range(BLK):
        parts[2 * j] = dot(coef[:, cols(j)].T, xs[BLK - 1 - j], NN).astype(BF)
        upstream = top[...] if j == BLK - 1 else grads[j + 1]
        parts[2 * j + 1] = dot(gates[:, cols(j)].T, upstream, NN).astype(BF)


def sum_kernel(parts, out):
    total = parts[0].astype(F32)
    for n in range(1, N):
        total = total + parts[n].astype(F32)
    out[...] = total


def whole(shape):
    return pl.BlockSpec(shape, lambda n: (0,) * len(shape))


def half(shape, at):
    return pl.BlockSpec(shape, lambda n: (at,) + (0,) * (len(shape) - 1))


def swap(block):
    return lax.all_to_all(block, "section", 0, 0, tiled=True)


def body(parked, cotangent, park_table, run_order, norm_gain, down_weight, up_weight):
    me = lax.axis_index("section")
    rep = lax.axis_index("dp")
    micro, rows, width = cotangent.shape

    gain = norm_gain[0].reshape(N, N, 32, 1)
    down = down_weight[0].reshape(N, N, 32, RANK)
    down = lax.dynamic_index_in_dim(down, rep, 1, keepdims=False).astype(F32)
    down = (down * lax.dynamic_index_in_dim(gain, rep, 1, keepdims=False)).astype(BF)
    up = lax.dynamic_slice_in_dim(up_weight[0], 16 * (rep // 2), 16, 0)
    up = lax.dynamic_index_in_dim(up.reshape(16, N, 2, 2, RANK), rep % 2, 2, keepdims=False)
    up = up.transpose(1, 2, 0, 3).reshape(N, 32, RANK)
    thin = lax.all_to_all(jnp.concatenate([up, down], axis=1), "section", 0, 0)
    big = lax.all_gather(thin, "dp")

    slot_row = lax.dynamic_index_in_dim(park_table, me, 0, keepdims=False)
    hit = (run_order[:, None] == slot_row[None, :]).astype(jnp.int32)
    slots = jnp.sum(hit * jnp.arange(micro, dtype=jnp.int32)[None, :], axis=1)
    xs = lax.all_to_all(split_rows(parked[0], slots), "section", 0, 0)
    cot = lax.dynamic_slice_in_dim(cotangent, me * F, F, 2)
    cot = jnp.take(cot, run_order, axis=0).reshape(ROWS, F)

    side = BLK * (rep // BLK)
    near = rep % BLK
    far = (near + jnp.arange(1, 5, dtype=jnp.int32)) % BLK
    smem = pl.BlockSpec(memory_space=pltpu.SMEM)
    vmem = pl.BlockSpec(memory_space=pltpu.VMEM)
    ups, downs, w_part = call(
        weight_kernel,
        [((N, RANK, F), BF), ((N, F, RANK), BF), ((4 * RANK, RANK), BF)],
        in_specs=[smem, smem, vmem],
    )(side + jnp.maximum(near, far), side + jnp.minimum(near, far), big)
    w_sum = swap(w_part).astype(F32).reshape(N, 4 * RANK // N, RANK).sum(0).astype(BF)
    w_all = swap(jnp.broadcast_to(w_sum[None], (N,) + w_sum.shape).reshape(4 * RANK, RANK))
    w_all = lax.all_gather(w_all, "dp")

    (pay1,) = call(
        functools.partial(cross_kernel, True), [((ROWS, (2 * BLK + NP + 1) * RANK), BF)]
    )(xs, ups, downs, cot)
    got1 = swap(pay1)
    (pay2,) = call(functools.partial(cross_kernel, False), [((ROWS, (BLK + NP) * RANK), BF)])(
        xs, ups, downs
    )
    got2 = swap(pay2)

    rank_outs = [((ROWS, (BLK + 1) * RANK), BF), ((ROWS, BLK * RANK), BF)]
    coef1, gates1 = call(functools.partial(rank_kernel, True), rank_outs)(got1, w_all)
    coef1 = swap(coef1)
    gates1 = swap(gates1)

    half_rows, half_down, half_up = (BLK, ROWS, F), (BLK, F, RANK), (BLK, RANK, F)
    grads1, pay3, carry = call(
        functools.partial(update_kernel, True),
        [((N, ROWS, F), BF), ((ROWS, BLK * RANK), BF), ((ROWS, F), F32)],
        grid=(1,),
        in_specs=[
            whole((ROWS, F)),
            whole(coef1.shape),
            half(half_rows, 0),
            half(half_down, 1),
            half(half_up, 0),
        ],
        out_specs=[half(half_rows, 1), whole((ROWS, BLK * RANK)), whole((ROWS, F))],
    )(cot, coef1, xs, downs, ups)
    got3 = swap(pay3)

    def weight_parts(coef, gates, xs_at, top, top_spec, grads, grads_at):
        (parts,) = call(
            parts_kernel,
            [((N, RANK, F), BF)],
            grid=(1,),
            in_specs=[
                whole(coef.shape),
                whole(gates.shape),
                half(half_rows, xs_at),
                top_spec,
                half(half_rows, grads_at),
            ],
            out_specs=[whole((N, RANK, F))],
        )(coef, gates, xs, top, grads)
        parts = lax.all_to_all(parts, "dp", 0, 0)
        (total,) = call(sum_kernel, [((RANK, F), F32)])(parts)
        return total

    total1 = weight_parts(coef1, gates1, 0, cot, whole((ROWS, F)), grads1, 1)

    power_spec = pl.BlockSpec((ROWS, RANK), lambda n: (0, 2 * BLK + NP))
    coef2, gates2 = call(
        functools.partial(rank_kernel, False),
        rank_outs,
        grid=(1,),
        in_specs=[whole(got3.shape), whole(got2.shape), power_spec, whole(w_all.shape)],
        out_specs=[whole(s) for s, _ in rank_outs],
    )(got3, got2, got1, w_all)
    coef2 = swap(coef2)
    gates2 = swap(gates2)
    (grads2,) = call(
        functools.partial(update_kernel, False),
        [((N, ROWS, F), BF)],
        grid=(1,),
        in_specs=[
            whole((ROWS, F)),
            whole(coef2.shape),
            half(half_rows, 1),
            half(half_down, 0),
            pl.BlockSpec(memory_space=pl.ANY),
        ],
        out_specs=[half(half_rows, 0)],
        input_output_aliases={4: 0},
    )(carry, coef2, xs, downs, grads1)
    out = join_rows(lax.all_to_all(grads2, "section", 0, 0), micro)

    top2 = pl.BlockSpec((None, ROWS, F), lambda n: (BLK, 0, 0))
    total2 = weight_parts(coef2, gates2, 1, grads2, top2, grads2, 0)

    def homeward(total, block, kind):
        route = [
            (f * N + 2 * t + kind, (BLK * block + t) * N + f) for f in range(N) for t in range(BLK)
        ]
        return lax.ppermute(total, ("section", "dp"), route)

    down_grad = homeward(total1, 1, 0) + homeward(total2, 0, 0)
    up_grad = homeward(total1, 1, 1) + homeward(total2, 0, 1)
    own_gain = lax.dynamic_slice_in_dim(norm_gain[0], rep * F, F, 0)
    return (out[None], (down_grad.T * own_gain[:, None])[None], up_grad[None])


def solution(mesh):
    placed = (
        P("section", None, "dp", None),
        P(None, "dp", None),
        P(),
        P(),
        P("section", None),
        P("section", None, None),
        P("section", None, None),
    )
    return jax.shard_map(
        body,
        mesh=mesh,
        in_specs=placed,
        out_specs=(
            P("section", None, "dp", None),
            P("section", "dp", None),
            P("section", None, "dp"),
        ),
        check_vma=False,
    )
```

time: 981 us -> 520 us (0.53)
  waiting for transfers between devices: 666 us -> 222 us
  blocking collectives: 0 us -> 145 us
  other arithmetic: 120 us -> 6.33 us
  matrix products: 88.4 us -> 0 us
  Pallas kernels: 0 us -> 52.4 us
  local copies, waits for them, and re-layouts: 49.9 us -> 7.12 us
  starting transfers between devices: 37.5 us -> 62.5 us
    ppermute x23 -> x4, waiting for transfers between devices: 482 us -> 76.3 us  [homeward(): return lax.ppermute(total, ('section', 'dp'), route)]
    psum x1 -> x0, waiting for transfers between devices: 184 us -> none  [body(): lax.psum(down_terms.astype(jnp.bfloat16), 'dp').astype(jnp.float32)]
    all_to_all x0 -> x6, blocking collectives: none -> 145 us  [the longest x4 93 us: swap(): return lax.all_to_all(block, 'section', 0, 0, tiled=True)]
    all_to_all x0 -> x8, waiting for transfers between devices: none -> 108 us  [the longest x1 45.3 us: body(): xs = lax.all_to_all(split_rows(parked[0], slots), 'section', 0, 0)]
    dynamic_update_slice x38 -> x0, other arithmetic: 94.1 us -> none  [store(): lax.dynamic_update_index_in_dim(buffer, jnp.where(active, new_value, prev...]
    dot_general x61 -> x0, matrix products: 88.4 us -> none  [the longest x19 43.2 us: layer_back(): pre_act = jnp.dot(hidden, down_local, preferred_element_type=jnp.float32)]
    pallas_call x0 -> x13, Pallas kernels: none -> 52.4 us  [the longest x2 7.69 us: weight_parts(): call(parts_kernel, [((N, RANK, F), BF)], grid=(1,), in_specs=[whole(coef....]
    all_to_all x0 -> x8, starting transfers between devices: none -> 47.3 us  [the longest x5 28.8 us: swap(): return lax.all_to_all(block, 'section', 0, 0, tiled=True)]
  transfers between devices with their start and end apart: 24 -> 14, of which waited for: 24 -> 9; matrix products, arithmetic and copies ran while one was open for 1% -> 1% of each run, Pallas kernels for 0% -> 8%
where the time goes in v1:
time: 520 us; the launch traced here: 510 us
  waiting for transfers between devices  222 us (43%)
  blocking collectives  145 us (28%)
  starting transfers between devices  62.5 us (12%)
  Pallas kernels  52.4 us (10%)
  between operations  14.4 us (3%)
  local copies, waits for them, and re-layouts  7.12 us (1%)
  other arithmetic  6.33 us (1%)
    all_to_all x4, blocking collectives, swap(): return lax.all_to_all(block, 'section', 0, 0, tiled=True)  93 us
    ppermute x4, waiting for transfers between devices, homeward(): return lax.ppermute(total, ('section', 'dp'), route)  76.3 us
    all_to_all x1, waiting for transfers between devices, body(): xs = lax.all_to_all(split_rows(parked[0], slots), 'section', 0, 0)  45.3 us
    all_to_all x5, waiting for transfers between devices, swap(): return lax.all_to_all(block, 'section', 0, 0, tiled=True)  45.2 us
    all_gather x1, waiting for transfers between devices, body(): big = lax.all_gather(thin, 'dp')  37 us
    all_to_all x1, blocking collectives, weight_parts(): parts = lax.all_to_all(parts, 'dp', 0, 0)  32.2 us
    all_to_all x5, starting transfers between devices, swap(): return lax.all_to_all(block, 'section', 0, 0, tiled=True)  28.8 us
    all_to_all x1, blocking collectives, body(): thin = lax.all_to_all(jnp.concatenate([up, down], axis=1), 'section', 0, 0)  20.2 us
  transfers between devices with their start and end apart: 14, of which 9 were waited for; matrix products, arithmetic and copies ran while one was open for 1% of the time, Pallas kernels for 8%

profile of v1, /device:TPU:15, one launch (start us, length us, event | category | flops | bytes accessed | tf_op | source)
XLA Modules:
  0.0 510.3 jit_solution(2634364659919036491)
XLA Ops:
  7.2 0.5 broadcast.46
  7.8 1.5 reduce.6
  9.3 0.1 reshape_squeeze.7
  9.4 0.2 reshape.61
  9.6 0.1 constant_dynamic-slice_fusion.2
  9.7 0.1 copy.26
  9.8 1.0 fusion
  10.9 20.2 %all_to_all.117 = bf16[16,64,128]{2,1,0:T(8,128)(2,1)} all-to-all(bf16[16,64,128]{2,1,0:T(8,128)(2,1)S(1)} %pad_maximum_fusion), channel_id=1, replica_groups=mesh['section'=16,'dp'=16] {'section'}, dimensions={0} | all-to-all | bytes 524288 | tf_op jit(solution)/shard_map/all_to_all | solution.py:222
  31.1 0.5 minimum_add_fusion
  31.6 37.0 %all-gather.6.cloned.1.call-done = bf16[256,64,128]{2,1,0:T(8,128)(2,1)} async-done(((bf16[16,64,128]{2,1,0:T(8,128)(2,1)}), bf16[256,64,128]{2,1,0:T(8,128)(2,1)}) %all-gather.6.cloned.1.call-update) | async-done | bytes 4194320 | tf_op jit(solution)/shard_map/all_gather | solution.py:223
  68.7 4.8 shard_map.95
  73.5 17.3 %all_to_all.118 = bf16[16,32,128]{2,1,0:T(8,128)(2,1)S(1)} all-to-all(bf16[16,32,128]{2,1,0:T(8,128)(2,1)} %bitcast.65), channel_id=1, replica_groups=mesh['section'=16,'dp'=16] {'section'}, dimensions={0} | all-to-all | bytes 262144 | tf_op jit(solution)/shard_map/all_to_all | solution.py:207
  90.8 0.7 broadcast_in_dim.40
  91.5 4.3 all-to-all-start.4
  95.8 0.2 dynamic-slice_reduce_fusion
  96.0 0.7 select_reduce_fusion.slots
  96.7 4.5 shard_map.94
  101.1 3.7 all-to-all-done.4
  104.8 0.7 copy-done.5
  105.5 5.4 %all-to-all-start = ((bf16[16,128,512]{2,1,0:T(8,128)(2,1)}), bf16[16,128,512]{2,1,0:T(8,128)(2,1)}, u32[]{:S(2)}, u32[]{:S(2)}) async-start(bf16[16,128,512]{2,1,0:T(8,128)(2,1)} %bitcast.44), calls=%async_computation | async-start | bytes 4194304 | tf_op jit(solution)/shard_map/all_to_all | solution.py:228
  110.9 0.0 all-gather.4.cloned.1.call-start
  111.0 0.7 all-gather.4.cloned.1.call-update
  111.7 0.1 broadcast_in_dim.35
  111.8 0.1 broadcast_in_dim.36
  111.9 0.9 constant_dynamic-slice_fusion.4
  112.8 0.6 gather_fusion
  113.3 0.7 bitcast_select_fusion.refs_0_.top
  114.1 45.3 %all-to-all-done.xs = bf16[16,128,512]{2,1,0:T(8,128)(2,1)} async-done(((bf16[16,128,512]{2,1,0:T(8,128)(2,1)}), bf16[16,128,512]{2,1,0:T(8,128)(2,1)}, u32[]{:S(2)}, u32[]{:S(2)}) %all-to-all-start) | async-done | bytes 2097184 | tf_op jit(solution)/shard_map/all_to_all | solution.py:228
  159.4 6.0 %shard_map.96 = bf16[128,5760]{1,0:T(8,128)(2,1)} custom-call(bf16[16,128,512]{2,1,0:T(8,128)(2,1)} %all-to-all-done.xs, bf16[16,128,512]{2,1,0:T(8,128)(2,1)} %get-tuple-element.13.up.refs_0_, bf16[16,512,128]{2,1,0:T(8,128)(2,1)} %get-tuple-element.14.down, bf16[128,512]{1,0:T(8,128)(2,1)} %bitcast_select_fusion.refs_0_.top), custom_call_target="tpu_custom_call" | custom-call | tf_op jit(solution)/shard_map/pallas_call | solution.py:246
  165.4 42.6 %all_to_all.119 = bf16[16,8,5760]{2,1,0:T(8,128)(2,1)} all-to-all(bf16[16,8,5760]{2,1,0:T(8,128)(2,1)} %bitcast.45), channel_id=1, replica_groups=mesh['section'=16,'dp'=16] {'section'}, dimensions={0} | all-to-all | bytes 2949120 | tf_op jit(solution)/shard_map/all_to_all | solution.py:207
  208.0 4.2 shard_map.97
  212.2 6.5 %all-to-all-start.5 = ((bf16[16,8,1152]{2,1,0:T(8,128)(2,1)}), bf16[16,8,1152]{2,1,0:T(8,128)(2,1)S(1)}, u32[]{:S(2)}, u32[]{:S(2)}) async-start(bf16[16,8,1152]{2,1,0:T(8,128)(2,1)} %bitcast.61), calls=%async_computation.5 | async-start | bytes 589824 | tf_op jit(solution)/shard_map/all_to_all | solution.py:207
  218.7 5.4 %shard_map.99 = bf16[128,4608]{1,0:T(8,128)(2,1)} custom-call(bf16[16,128,512]{2,1,0:T(8,128)(2,1)} %all-to-all-done.xs, bf16[16,128,512]{2,1,0:T(8,128)(2,1)} %get-tuple-element.13.up.refs_0_, bf16[16,512,128]{2,1,0:T(8,128)(2,1)} %get-tuple-element.14.down), custom_call_target="tpu_custom_call" | custom-call | tf_op jit(solution)/shard_map/pallas_call | solution.py:250
  224.1 4.7 all-to-all-done.5
  228.8 0.7 copy-done.3
  229.6 6.1 %all-to-all-start.7 = ((bf16[16,8,4608]{2,1,0:T(8,128)(2,1)}), bf16[16,8,4608]{2,1,0:T(8,128)(2,1)S(1)}, u32[]{:S(2)}, u32[]{:S(2)}) async-start(bf16[16,8,4608]{2,1,0:T(8,128)(2,1)} %bitcast.47), calls=%async_computation.7 | async-start | bytes 2359296 | tf_op jit(solution)/shard_map/all_to_all | solution.py:207
  235.7 3.6 shard_map.98
  239.3 25.3 %all-to-all-done.7 = bf16[16,8,4608]{2,1,0:T(8,128)(2,1)S(1)} async-done(((bf16[16,8,4608]{2,1,0:T(8,128)(2,1)}), bf16[16,8,4608]{2,1,0:T(8,128)(2,1)S(1)}, u32[]{:S(2)}, u32[]{:S(2)}) %all-to-all-start.7) | async-done | bytes 1179680 | tf_op jit(solution)/shard_map/all_to_all | solution.py:207
  264.7 17.4 %all_to_all.120 = bf16[16,8,1024]{2,1,0:T(8,128)(2,1)} all-to-all(bf16[16,8,1024]{2,1,0:T(8,128)(2,1)} %bitcast.64), channel_id=1, replica_groups=mesh['section'=16,'dp'=16] {'section'}, dimensions={0} | all-to-all | bytes 524288 | tf_op jit(solution)/shard_map/all_to_all | solution.py:207
  282.0 5.6 %all-to-all-start.10 = ((bf16[16,8,1024]{2,1,0:T(8,128)(2,1)}), bf16[16,8,1024]{2,1,0:T(8,128)(2,1)S(1)}, u32[]{:S(2)}, u32[]{:S(2)}) async-start(bf16[16,8,1024]{2,1,0:T(8,128)(2,1)} %bitcast.62), calls=%async_computation.10 | async-start | bytes 524288 | tf_op jit(solution)/shard_map/all_to_all | solution.py:207
  287.7 4.2 shard_map.100
  291.8 5.2 %all-to-all-done.10 = bf16[16,8,1024]{2,1,0:T(8,128)(2,1)S(1)} async-done(((bf16[16,8,1024]{2,1,0:T(8,128)(2,1)}), bf16[16,8,1024]{2,1,0:T(8,128)(2,1)S(1)}, u32[]{:S(2)}, u32[]{:S(2)}) %all-to-all-start.10) | async-done | bytes 262176 | tf_op jit(solution)/shard_map/all_to_all | solution.py:207
  297.0 15.7 %all_to_all.121 = bf16[16,8,1024]{2,1,0:T(8,128)(2,1)} all-to-all(bf16[16,8,1024]{2,1,0:T(8,128)(2,1)} %bitcast.63), channel_id=1, replica_groups=mesh['section'=16,'dp'=16] {'section'}, dimensions={0} | all-to-all | bytes 524288 | tf_op jit(solution)/shard_map/all_to_all | solution.py:207
  312.7 6.3 %all-to-all-start.8 = ((bf16[16,8,1152]{2,1,0:T(8,128)(2,1)}), bf16[16,8,1152]{2,1,0:T(8,128)(2,1)S(1)}, u32[]{:S(2)}, u32[]{:S(2)}) async-start(bf16[16,8,1152]{2,1,0:T(8,128)(2,1)} %bitcast.60), calls=%async_computation.8 | async-start | bytes 589824 | tf_op jit(solution)/shard_map/all_to_all | solution.py:207
  319.0 3.8 shard_map.103
  322.9 6.3 %all-to-all-done.8 = bf16[16,8,1152]{2,1,0:T(8,128)(2,1)S(1)} async-done(((bf16[16,8,1152]{2,1,0:T(8,128)(2,1)}), bf16[16,8,1152]{2,1,0:T(8,128)(2,1)S(1)}, u32[]{:S(2)}, u32[]{:S(2)}) %all-to-all-start.8) | async-done | bytes 294944 | tf_op jit(solution)/shard_map/all_to_all | solution.py:207
  329.2 0.7 copy-done.2
  329.9 8.5 %all-to-all-start.11 = ((bf16[16,128,512]{2,1,0:T(8,128)(2,1)}), bf16[16,128,512]{2,1,0:T(8,128)(2,1)}, u32[]{:S(2)}, u32[]{:S(2)}) async-start(bf16[16,128,512]{2,1,0:T(8,128)(2,1)} %shard_map.103), calls=%async_computation.11 | async-start | bytes 4194304 | tf_op jit(solution)/shard_map/all_to_all | solution.py:290
  338.4 3.2 shard_map.101.top.grads
  341.6 3.9 shard_map.105
  345.5 17.7 %all-to-all-done.11.parts = bf16[16,128,512]{2,1,0:T(8,128)(2,1)} async-done(((bf16[16,128,512]{2,1,0:T(8,128)(2,1)}), bf16[16,128,512]{2,1,0:T(8,128)(2,1)}, u32[]{:S(2)}, u32[]{:S(2)}) %all-to-all-start.11) | async-done | bytes 2097184 | tf_op jit(solution)/shard_map/all_to_all | solution.py:290
  363.1 32.2 %all_to_all.122.parts = bf16[16,128,512]{2,1,0:T(8,128)(2,1)} all-to-all(bf16[16,128,512]{2,1,0:T(8,128)(2,1)} %shard_map.105), channel_id=1, replica_groups=mesh['section'=16,'dp'=16] {'dp'}, dimensions={0} | all-to-all | bytes 4194304 | tf_op jit(solution)/shard_map/all_to_all | solution.py:290
  395.4 4.5 all-to-all-start.9
  399.9 2.6 shard_map.104
  402.4 0.8 collective-permute-start
  403.2 2.6 shard_map.106
  405.8 1.3 collective-permute-start.1
  407.1 11.1 %collective-permute-start.2 = (f32[128,512]{1,0:T(8,128)S(1)}, f32[128,512]{1,0:T(8,128)S(1)}, u32[]{:S(2)}, u32[]{:S(2)}) collective-permute-start(f32[128,512]{1,0:T(8,128)S(1)} %copy-done.6), channel_id=1, source_target_pairs={{1,128},{3,144},{5,160},{7,176},{9,192},{11,208},{13,224},{15,240}... | collective-permute-start | bytes 786440 | tf_op jit(solution)/shard_map/ppermute | solution.py:329
  418.3 1.9 collective-permute-start.3
  420.2 0.7 constant_dynamic-slice_fusion
  420.9 76.3 %collective-permute-done.1 = f32[128,512]{1,0:T(8,128)S(1)} collective-permute-done((f32[128,512]{1,0:T(8,128)}, f32[128,512]{1,0:T(8,128)S(1)}, u32[]{:S(2)}, u32[]{:S(2)}) %collective-permute-start.1) | collective-permute-done | bytes 262176 | tf_op jit(solution)/shard_map/ppermute | solution.py:329
  497.2 0.8 copy.25
  498.0 1.7 add_bitcast_fusion
  499.7 3.8 shard_map.102
  (30 shorter events, 0.2 us)
Async XLA Ops:
  7.2 2.2 copy-start
  7.2 61.5 %all-gather.6.cloned.1.call-start = ((), (), s32[]{:S(2)}) async-start(), calls=%async_computation.15 | async-start | bytes 4456448 | tf_op jit(solution)/shard_map/all_gather | solution.py:223
  68.7 27.1 %copy-start.7 = (s32[16,4]{0,1:T(4,128)S(1)}, s32[16,4]{0,1:T(4,128)}, u32[]{:S(2)}) copy-start(s32[16,4]{0,1:T(4,128)} %param.9) | copy-start | bytes 772
  68.7 27.3 %copy-start.8 = (s32[4]{0:T(128)S(1)}, s32[4]{0:T(128)}, u32[]{:S(2)}) copy-start(s32[4]{0:T(128)} %param.10) | copy-start | bytes 52
  91.5 13.3 %all-to-all-start.4 = ((bf16[16,32,128]{2,1,0:T(8,128)(2,1)}), bf16[16,32,128]{2,1,0:T(8,128)(2,1)S(1)}, u32[]{:S(2)}, u32[]{:S(2)}) async-start(bf16[16,32,128]{2,1,0:T(8,128)(2,1)} %broadcast_in_dim.40), calls=%async_computation.4 | async-start | bytes 262144 | tf_op jit(solution)/shard_map/all_to_all | solution.py:207
  104.8 0.7 copy-start.5
  105.5 54.0 %all-to-all-start = ((bf16[16,128,512]{2,1,0:T(8,128)(2,1)}), bf16[16,128,512]{2,1,0:T(8,128)(2,1)}, u32[]{:S(2)}, u32[]{:S(2)}) async-start(bf16[16,128,512]{2,1,0:T(8,128)(2,1)} %bitcast.44), calls=%async_computation | async-start | bytes 4194304 | tf_op jit(solution)/shard_map/all_to_all | solution.py:228
  110.9 97.1 %all-gather.4.cloned.1.call-start = ((), (), s32[]{:S(2)}) async-start(), calls=%async_computation.14 | async-start | bytes 2228224 | tf_op jit(solution)/shard_map/all_gather | solution.py:244
  212.2 16.7 %all-to-all-start.5 = ((bf16[16,8,1152]{2,1,0:T(8,128)(2,1)}), bf16[16,8,1152]{2,1,0:T(8,128)(2,1)S(1)}, u32[]{:S(2)}, u32[]{:S(2)}) async-start(bf16[16,8,1152]{2,1,0:T(8,128)(2,1)} %bitcast.61), calls=%async_computation.5 | async-start | bytes 589824 | tf_op jit(solution)/shard_map/all_to_all | solution.py:207
  228.8 0.7 copy-start.3
  229.6 35.1 %all-to-all-start.7 = ((bf16[16,8,4608]{2,1,0:T(8,128)(2,1)}), bf16[16,8,4608]{2,1,0:T(8,128)(2,1)S(1)}, u32[]{:S(2)}, u32[]{:S(2)}) async-start(bf16[16,8,4608]{2,1,0:T(8,128)(2,1)} %bitcast.47), calls=%async_computation.7 | async-start | bytes 2359296 | tf_op jit(solution)/shard_map/all_to_all | solution.py:207
  264.7 23.0 %copy-start.1 = (bf16[16,8,4608]{2,1,0:T(8,128)(2,1)}, bf16[16,8,4608]{2,1,0:T(8,128)(2,1)S(1)}, u32[]{:S(2)}) copy-start(bf16[16,8,4608]{2,1,0:T(8,128)(2,1)S(1)} %all-to-all-done.7) | copy-start | bytes 3538948
  282.0 15.0 %all-to-all-start.10 = ((bf16[16,8,1024]{2,1,0:T(8,128)(2,1)}), bf16[16,8,1024]{2,1,0:T(8,128)(2,1)S(1)}, u32[]{:S(2)}, u32[]{:S(2)}) async-start(bf16[16,8,1024]{2,1,0:T(8,128)(2,1)} %bitcast.62), calls=%async_computation.10 | async-start | bytes 524288 | tf_op jit(solution)/shard_map/all_to_all | solution.py:207
  297.0 22.0 %copy-start.4 = (bf16[16,8,1024]{2,1,0:T(8,128)(2,1)}, bf16[16,8,1024]{2,1,0:T(8,128)(2,1)S(1)}, u32[]{:S(2)}) copy-start(bf16[16,8,1024]{2,1,0:T(8,128)(2,1)S(1)} %all-to-all-done.10) | copy-start | bytes 786436
  312.7 16.4 %all-to-all-start.8 = ((bf16[16,8,1152]{2,1,0:T(8,128)(2,1)}), bf16[16,8,1152]{2,1,0:T(8,128)(2,1)S(1)}, u32[]{:S(2)}, u32[]{:S(2)}) async-start(bf16[16,8,1152]{2,1,0:T(8,128)(2,1)} %bitcast.60), calls=%async_computation.8 | async-start | bytes 589824 | tf_op jit(solution)/shard_map/all_to_all | solution.py:207
  329.2 0.7 copy-start.2
  329.9 33.2 %all-to-all-start.11 = ((bf16[16,128,512]{2,1,0:T(8,128)(2,1)}), bf16[16,128,512]{2,1,0:T(8,128)(2,1)}, u32[]{:S(2)}, u32[]{:S(2)}) async-start(bf16[16,128,512]{2,1,0:T(8,128)(2,1)} %shard_map.103), calls=%async_computation.11 | async-start | bytes 4194304 | tf_op jit(solution)/shard_map/all_to_all | solution.py:290
  395.4 104.4 %all-to-all-start.9 = ((bf16[16,128,512]{2,1,0:T(8,128)(2,1)}), bf16[16,128,512]{2,1,0:T(8,128)(2,1)}, u32[]{:S(2)}, u32[]{:S(2)}) async-start(bf16[16,128,512]{2,1,0:T(8,128)(2,1)} %shard_map.101.top.grads), calls=%async_computation.9 | async-start | bytes 4194304 | tf_op jit(solution)/shard_map/all_to_all | solution.py:320
  402.4 4.7 copy-start.6
  402.4 18.4 %collective-permute-start = (f32[128,512]{1,0:T(8,128)}, f32[128,512]{1,0:T(8,128)S(1)}, u32[]{:S(2)}, u32[]{:S(2)}) collective-permute-start(f32[128,512]{1,0:T(8,128)} %shard_map.104), channel_id=1, source_target_pairs={{0,128},{2,144},{4,160},{6,176},{8,192},{10,208},{12,224},{14,240}... | collective-permute-start | bytes 786440 | tf_op jit(solution)/shard_map/ppermute | solution.py:329
  405.8 91.3 %collective-permute-start.1 = (f32[128,512]{1,0:T(8,128)}, f32[128,512]{1,0:T(8,128)S(1)}, u32[]{:S(2)}, u32[]{:S(2)}) collective-permute-start(f32[128,512]{1,0:T(8,128)} %shard_map.106), channel_id=1, source_target_pairs={{0,0},{2,16},{4,32},{6,48},{8,64},{10,80},{12,96},{14,112},{16,1},... | collective-permute-start | bytes 786440 | tf_op jit(solution)/shard_map/ppermute | solution.py:329
  407.1 90.9 %collective-permute-start.2 = (f32[128,512]{1,0:T(8,128)S(1)}, f32[128,512]{1,0:T(8,128)S(1)}, u32[]{:S(2)}, u32[]{:S(2)}) collective-permute-start(f32[128,512]{1,0:T(8,128)S(1)} %copy-done.6), channel_id=1, source_target_pairs={{1,128},{3,144},{5,160},{7,176},{9,192},{11,208},{13,224},{15,240}... | collective-permute-start | bytes 786440 | tf_op jit(solution)/shard_map/ppermute | solution.py:329
  418.3 79.8 %collective-permute-start.3 = (f32[128,512]{1,0:T(8,128)}, f32[128,512]{1,0:T(8,128)}, u32[]{:S(2)}, u32[]{:S(2)}) collective-permute-start(f32[128,512]{1,0:T(8,128)} %shard_map.106), channel_id=1, source_target_pairs={{1,0},{3,16},{5,32},{7,48},{9,64},{11,80},{13,96},{15,112},{17,1},... | collective-permute-start | bytes 786440 | tf_op jit(solution)/shard_map/ppermute | solution.py:329
Sparse Core Ops, SparseCore 0:
  31.2 37.4 all-gather.5
  114.2 41.8 all-gather.3
